TPU v7x, 32 devices: a whole 2x2x4 slice. The times are simulated.
32 devices in a mesh: grp: 2 (over y), tile: 8 (over z, x), tm: 2 (over core).
Axes of the slice: x: 2, y: 2, z: 4, core: 2. Of those that a mesh axis runs over, the one named last changes fastest.
Arguments:
- video: bfloat16 [8, 16, 256, 128], P(('grp', 'tm'), 'tile'), parts along dimension 0, may hold values from -60 to 60
- conv_first: bfloat16 [3, 3, 3, 128, 128], replicated, may hold values from -0.109375 to 0.109375
- conv_second: bfloat16 [3, 3, 3, 128, 128], replicated, may hold values from -0.109375 to 0.109375
- gain_first: float32 [128], replicated, may hold values from 0.1 to 1.9
- shift_first: float32 [128], replicated, may hold values from -3 to 3
- gain_second: float32 [128], replicated, may hold values from 0.1 to 1.9
- shift_second: float32 [128], replicated, may hold values from -3 to 3
- bias_second: float32 [128], replicated, may hold values from -3 to 3
Outputs:
- encoded: bfloat16 [8, 16, 256, 128], P(('grp', 'tm'), 'tile'), parts along dimension 0
There are 2 independent parts, one for each index of `grp`. A program takes and returns all parts, laid end to end along the dimension named above; an argument that names none is the same for every part. Nothing has to cross between parts.
All inputs are finite; a program needn't handle non-finite values.
Results may differ from a plain program's by a relative error of at most 0.002.
Values may be sent and summed in bfloat16 or wider, within the bound.
A program may use at most 64 MiB of HBM per device.

v0:
```python
import jax
import jax.numpy as jnp
from jax import lax
from jax.sharding import PartitionSpec as P

G = 32


EPSILON = 1e-06


def passed_along(x, axis, by):
    devices = lax.axis_size(axis)
    pairs = [(i, i + by) for i in range(devices) if 0 <= i + by < devices]
    return lax.ppermute(x, axis, pairs)


def extended_2(cells, sides, width):
    for axis, dim in sides:
        count = lax.axis_size(axis)
        ends = count - 1
        head = lax.slice_in_dim(cells, 0, width, axis=dim)
        tail = lax.slice_in_dim(cells, cells.shape[dim] - width, cells.shape[dim], axis=dim)
        cells = jnp.concatenate(
            [
                lax.ppermute(tail, axis, [(i, (i + 1) % count) for i in range(ends)]),
                cells,
                lax.ppermute(head, axis, [((i + 1) % count, i) for i in range(ends)]),
            ],
            axis=dim,
        )
    return cells


def norm_stats(values, cells_group):
    channels = values.shape[-1]
    flat = values.reshape(-1, channels)
    sums = jnp.sum(flat, axis=0).reshape(G, channels // G).sum(axis=1)
    squares = jnp.sum(flat * flat, axis=0).reshape(G, channels // G).sum(axis=1)
    totals, square_sums = lax.psum((sums, squares), ("tile", "tm"))
    center_mean = totals / cells_group
    spread = square_sums / cells_group - center_mean * center_mean
    return (center_mean, spread)


def normalize(values, center_mean, spread, gain, offset):
    channels = values.shape[-1]
    scale_group = lax.rsqrt(spread + EPSILON)
    mean_chan = jnp.repeat(center_mean, channels // G)
    scale_chan = jnp.repeat(scale_group, channels // G)
    normed = (values - mean_chan) * scale_chan * gain + offset
    return jax.nn.silu(normed).astype(jnp.bfloat16)


def causal_extend(block, received):
    front_frame = block[:1]
    repeated = jnp.concatenate([front_frame, front_frame], axis=0)
    history = jnp.where(lax.axis_index("tm") == 0, repeated, received)
    return jnp.concatenate([history, block], axis=0)


def conv_block(extended, weight):
    frame_count = extended.shape[0] - 2
    row_count = extended.shape[1] - 2
    col_count = extended.shape[2]
    channels = extended.shape[3]
    padded = jnp.pad(extended, ((0, 0), (0, 0), (1, 1), (0, 0)))
    accumulated = jnp.zeros((frame_count, row_count, col_count, weight.shape[-1]), jnp.float32)
    for time_tap in range(3):
        for row_tap in range(3):
            window = padded[time_tap : time_tap + frame_count, row_tap : row_tap + row_count]
            stacked = jnp.concatenate(
                [window[:, :, col_tap : col_tap + col_count] for col_tap in range(3)], axis=-1
            )
            kernel = weight[time_tap, row_tap].reshape(3 * channels, weight.shape[-1])
            accumulated = accumulated + jnp.dot(stacked, kernel, preferred_element_type=jnp.float32)
    return accumulated


def per_device(
    video, conv_first, conv_second, gain_first, shift_first, gain_second, shift_second, bias_second
):
    span_len, row_count, col_count, channels = video.shape
    cells_group = float(
        span_len
        * lax.axis_size("tm")
        * row_count
        * lax.axis_size("tile")
        * col_count
        * (channels // G)
    )
    source = video.astype(jnp.float32)
    mean_first, spread_first = norm_stats(source, cells_group)
    hidden_first = normalize(source, mean_first, spread_first, gain_first, shift_first)
    extended = causal_extend(hidden_first, passed_along(hidden_first, "tm", 1))
    first_out = conv_block(extended_2(extended, (("tile", 1),), 1), conv_first)
    mean_second, spread_second = norm_stats(first_out, cells_group)
    hidden_second = normalize(first_out, mean_second, spread_second, gain_second, shift_second)
    second_ext = causal_extend(hidden_second, passed_along(hidden_second, "tm", 1))
    branch = conv_block(extended_2(second_ext, (("tile", 1),), 1), conv_second)
    return (source + branch + bias_second).astype(jnp.bfloat16)


def solution(mesh):
    in_specs = (P(("grp", "tm"), "tile", None, None), P(), P(), P(), P(), P(), P(), P())
    out_specs = P(("grp", "tm"), "tile", None, None)
    return jax.shard_map(
        per_device, mesh=mesh, in_specs=in_specs, out_specs=out_specs, check_vma=False
    )
```

profile of v0, /device:TPU:3, one launch (start us, length us, event | category | flops | bytes accessed | tf_op | source)
XLA Modules:
  0.0 111.9 jit_solution(9301883458631496210)
XLA Ops:
  0.0 1.1 convert_reduce_fusion
  1.5 25.3 %all-reduce.3 = (f32[32]{0:T(128)S(1)}, f32[32]{0:T(128)S(1)}) all-reduce(f32[32]{0:T(128)S(1)} %reduce_sum.75, f32[32]{0:T(128)S(1)} %reduce_sum.73), channel_id=1, replica_groups=mesh['grp'=2,'tile'=8,'tm'=2] {'tile','tm'}, use_global_device_ids=true, to_apply=%region_5.0 | all-reduce | flops 64 | bytes 512 | tf_op jit(solution)/shard_map/psum | solution.py:40
  27.2 1.2 %fusion.116 = bf16[2,2,256,128]{3,2,1,0:T(8,128)(2,1)S(1)} fusion(bf16[2,2,256,128]{3,2,1,0:T(8,128)(2,1)} %param.8, f32[128]{0:T(128)} %param.12, f32[128]{0:T(128)} %param.11, f32[128]{0:T(128)S(1)} %mul.59, f32[128]{0:T(128)S(1)} %sub.26), kind=kLoop, calls=%fused_computation.151 | loop fusion | flops 1310720 | bytes 526336 | tf_op jit(solution)/shard_map/convert_element_type | solution.py:52
  28.4 1.4 %collective-permute-start = (bf16[2,2,256,128]{3,2,1,0:T(8,128)(2,1)S(1)}, bf16[2,2,256,128]{3,2,1,0:T(8,128)(2,1)S(1)}, u32[]{:S(2)}, u32[]{:S(2)}) collective-permute-start(bf16[2,2,256,128]{3,2,1,0:T(8,128)(2,1)S(1)} %fusion.116), channel_id=1, source_target_pairs={{0,1},{2,3},{4,5},{6,7},{8,9},{10,11},{12,13},{14,15},{16,17},{18,... | collective-permute-start | bytes 786440 | tf_op jit(solution)/shard_map/ppermute | solution.py:15
  29.9 5.4 %collective-permute-done = bf16[2,2,256,128]{3,2,1,0:T(8,128)(2,1)S(1)} collective-permute-done((bf16[2,2,256,128]{3,2,1,0:T(8,128)(2,1)S(1)}, bf16[2,2,256,128]{3,2,1,0:T(8,128)(2,1)S(1)}, u32[]{:S(2)}, u32[]{:S(2)}) %collective-permute-start) | collective-permute-done | bytes 262176 | tf_op jit(solution)/shard_map/ppermute | solution.py:15
  35.3 1.9 %collective-permute-start.1 = (bf16[4,1,256,128]{3,2,1,0:T(8,128)(2,1)S(1)}, bf16[4,1,256,128]{3,2,1,0:T(8,128)(2,1)S(1)}, u32[]{:S(2)}, u32[]{:S(2)}) collective-permute-start(bf16[4,1,256,128]{3,2,1,0:T(8,128)(2,1)S(1)} %get-tuple-element.85), channel_id=1, source_target_pairs={{0,2},{2,4},{4,6},{6,8},{8,10},{10,12},{12,14},{1,3},{3,5},{5,7},{... | collective-permute-start | bytes 786440 | tf_op jit(solution)/shard_map/ppermute | solution.py:26
  37.3 6.0 %collective-permute-start.2 = (bf16[4,1,256,128]{3,2,1,0:T(8,128)(2,1)S(1)}, bf16[4,1,256,128]{3,2,1,0:T(8,128)(2,1)S(1)}, u32[]{:S(2)}, u32[]{:S(2)}) collective-permute-start(bf16[4,1,256,128]{3,2,1,0:T(8,128)(2,1)S(1)} %get-tuple-element.86), channel_id=1, source_target_pairs={{2,0},{4,2},{6,4},{8,6},{10,8},{12,10},{14,12},{3,1},{5,3},{7,5},{... | collective-permute-start | bytes 786440 | tf_op jit(solution)/shard_map/ppermute | solution.py:28
  43.3 10.1 %collective-permute-done.1 = bf16[4,1,256,128]{3,2,1,0:T(8,128)(2,1)S(1)} collective-permute-done((bf16[4,1,256,128]{3,2,1,0:T(8,128)(2,1)S(1)}, bf16[4,1,256,128]{3,2,1,0:T(8,128)(2,1)S(1)}, u32[]{:S(2)}, u32[]{:S(2)}) %collective-permute-start.1) | collective-permute-done | bytes 262176 | tf_op jit(solution)/shard_map/ppermute | solution.py:26
  53.8 1.0 fusion.142
  55.2 0.4 fusion.22
  55.5 0.4 convolution_add_fusion.15
  55.9 0.4 convolution_add_fusion.14
  56.7 0.4 convolution_add_fusion.12
  57.8 0.4 convolution_add_fusion.9
  58.2 0.4 fusion.140
  59.1 24.1 %all-reduce.2 = (f32[32]{0:T(128)S(1)}, f32[32]{0:T(128)S(1)}) all-reduce(f32[32]{0:T(128)S(1)} %reduce_sum.79, f32[32]{0:T(128)S(1)} %reduce_sum.77), channel_id=1, replica_groups=mesh['grp'=2,'tile'=8,'tm'=2] {'tile','tm'}, use_global_device_ids=true, to_apply=%region_11.12 | all-reduce | flops 64 | bytes 512 | tf_op jit(solution)/shard_map/psum | solution.py:40
  83.8 1.4 %collective-permute-start.3 = (bf16[2,2,256,128]{3,2,1,0:T(8,128)(2,1)S(1)}, bf16[2,2,256,128]{3,2,1,0:T(8,128)(2,1)S(1)}, u32[]{:S(2)}, u32[]{:S(2)}) collective-permute-start(bf16[2,2,256,128]{3,2,1,0:T(8,128)(2,1)S(1)} %multiply_convert_fusion), channel_id=1, source_target_pairs={{0,1},{2,3},{4,5},{6,7},{8,9},{10,11},{12,13},{14,15},{16,17},{18,... | collective-permute-start | bytes 786440 | tf_op jit(solution)/shard_map/ppermute | solution.py:15
  85.2 2.1 %collective-permute-done.3 = bf16[2,2,256,128]{3,2,1,0:T(8,128)(2,1)S(1)} collective-permute-done((bf16[2,2,256,128]{3,2,1,0:T(8,128)(2,1)S(1)}, bf16[2,2,256,128]{3,2,1,0:T(8,128)(2,1)S(1)}, u32[]{:S(2)}, u32[]{:S(2)}) %collective-permute-start.3) | collective-permute-done | bytes 262176 | tf_op jit(solution)/shard_map/ppermute | solution.py:15
  87.4 1.9 %collective-permute-start.4 = (bf16[4,1,256,128]{3,2,1,0:T(8,128)(2,1)S(1)}, bf16[4,1,256,128]{3,2,1,0:T(8,128)(2,1)S(1)}, u32[]{:S(2)}, u32[]{:S(2)}) collective-permute-start(bf16[4,1,256,128]{3,2,1,0:T(8,128)(2,1)S(1)} %get-tuple-element.81), channel_id=1, source_target_pairs={{0,2},{2,4},{4,6},{6,8},{8,10},{10,12},{12,14},{1,3},{3,5},{5,7},{... | collective-permute-start | bytes 786440 | tf_op jit(solution)/shard_map/ppermute | solution.py:26
  89.4 6.0 %collective-permute-start.5 = (bf16[4,1,256,128]{3,2,1,0:T(8,128)(2,1)S(1)}, bf16[4,1,256,128]{3,2,1,0:T(8,128)(2,1)S(1)}, u32[]{:S(2)}, u32[]{:S(2)}) collective-permute-start(bf16[4,1,256,128]{3,2,1,0:T(8,128)(2,1)S(1)} %get-tuple-element.82), channel_id=1, source_target_pairs={{2,0},{4,2},{6,4},{8,6},{10,8},{12,10},{14,12},{3,1},{5,3},{7,5},{... | collective-permute-start | bytes 786440 | tf_op jit(solution)/shard_map/ppermute | solution.py:28
  95.4 10.1 %collective-permute-done.4 = bf16[4,1,256,128]{3,2,1,0:T(8,128)(2,1)S(1)} collective-permute-done((bf16[4,1,256,128]{3,2,1,0:T(8,128)(2,1)S(1)}, bf16[4,1,256,128]{3,2,1,0:T(8,128)(2,1)S(1)}, u32[]{:S(2)}, u32[]{:S(2)}) %collective-permute-start.4) | collective-permute-done | bytes 262176 | tf_op jit(solution)/shard_map/ppermute | solution.py:26
  106.1 1.0 fusion.141
  107.2 0.4 fusion.65
  107.6 0.4 convolution_add_fusion.7
  108.0 0.4 convolution_add_fusion.6
  108.3 0.4 convolution_add_fusion.5
  108.7 0.4 convolution_add_fusion.4
  109.1 0.4 convolution_add_fusion.3
  109.5 0.4 convolution_add_fusion.2
  109.9 0.4 convolution_add_fusion.1
  110.2 0.6 copy-done
  110.8 1.1 fusion.3
  (50 shorter events, 4.5 us)
Async XLA Ops:
  28.4 14.9 %copy-start.1 = (bf16[3,3,3,128,128]{4,3,2,1,0:T(8,128)(2,1)S(1)}, bf16[3,3,3,128,128]{4,3,2,1,0:T(8,128)(2,1)}, u32[]{:S(2)}) copy-start(bf16[3,3,3,128,128]{4,3,2,1,0:T(8,128)(2,1)} %param.9) | copy-start | bytes 2654212
  28.4 6.8 %collective-permute-start = (bf16[2,2,256,128]{3,2,1,0:T(8,128)(2,1)S(1)}, bf16[2,2,256,128]{3,2,1,0:T(8,128)(2,1)S(1)}, u32[]{:S(2)}, u32[]{:S(2)}) collective-permute-start(bf16[2,2,256,128]{3,2,1,0:T(8,128)(2,1)S(1)} %fusion.116), channel_id=1, source_target_pairs={{0,1},{2,3},{4,5},{6,7},{8,9},{10,11},{12,13},{14,15},{16,17},{18,... | collective-permute-start | bytes 786440 | tf_op jit(solution)/shard_map/ppermute | solution.py:15
  35.3 18.1 %collective-permute-start.1 = (bf16[4,1,256,128]{3,2,1,0:T(8,128)(2,1)S(1)}, bf16[4,1,256,128]{3,2,1,0:T(8,128)(2,1)S(1)}, u32[]{:S(2)}, u32[]{:S(2)}) collective-permute-start(bf16[4,1,256,128]{3,2,1,0:T(8,128)(2,1)S(1)} %get-tuple-element.85), channel_id=1, source_target_pairs={{0,2},{2,4},{4,6},{6,8},{8,10},{10,12},{12,14},{1,3},{3,5},{5,7},{... | collective-permute-start | bytes 786440 | tf_op jit(solution)/shard_map/ppermute | solution.py:26
  37.3 16.2 %collective-permute-start.2 = (bf16[4,1,256,128]{3,2,1,0:T(8,128)(2,1)S(1)}, bf16[4,1,256,128]{3,2,1,0:T(8,128)(2,1)S(1)}, u32[]{:S(2)}, u32[]{:S(2)}) collective-permute-start(bf16[4,1,256,128]{3,2,1,0:T(8,128)(2,1)S(1)} %get-tuple-element.86), channel_id=1, source_target_pairs={{2,0},{4,2},{6,4},{8,6},{10,8},{12,10},{14,12},{3,1},{5,3},{7,5},{... | collective-permute-start | bytes 786440 | tf_op jit(solution)/shard_map/ppermute | solution.py:28
  58.2 25.4 %copy-start.3 = (f32[128]{0:T(128)S(1)}, f32[128]{0:T(128)}, u32[]{:S(2)}) copy-start(f32[128]{0:T(128)} %param.14) | copy-start | bytes 1540
  58.2 25.4 %copy-start.4 = (f32[128]{0:T(128)S(1)}, f32[128]{0:T(128)}, u32[]{:S(2)}) copy-start(f32[128]{0:T(128)} %param.13) | copy-start | bytes 1540
  83.8 11.6 %copy-start.2 = (bf16[3,3,3,128,128]{4,3,2,1,0:T(8,128)(2,1)S(1)}, bf16[3,3,3,128,128]{4,3,2,1,0:T(8,128)(2,1)}, u32[]{:S(2)}) copy-start(bf16[3,3,3,128,128]{4,3,2,1,0:T(8,128)(2,1)} %param.10) | copy-start | bytes 2654212
  83.8 3.6 %collective-permute-start.3 = (bf16[2,2,256,128]{3,2,1,0:T(8,128)(2,1)S(1)}, bf16[2,2,256,128]{3,2,1,0:T(8,128)(2,1)S(1)}, u32[]{:S(2)}, u32[]{:S(2)}) collective-permute-start(bf16[2,2,256,128]{3,2,1,0:T(8,128)(2,1)S(1)} %multiply_convert_fusion), channel_id=1, source_target_pairs={{0,1},{2,3},{4,5},{6,7},{8,9},{10,11},{12,13},{14,15},{16,17},{18,... | collective-permute-start | bytes 786440 | tf_op jit(solution)/shard_map/ppermute | solution.py:15
  87.4 18.1 %collective-permute-start.4 = (bf16[4,1,256,128]{3,2,1,0:T(8,128)(2,1)S(1)}, bf16[4,1,256,128]{3,2,1,0:T(8,128)(2,1)S(1)}, u32[]{:S(2)}, u32[]{:S(2)}) collective-permute-start(bf16[4,1,256,128]{3,2,1,0:T(8,128)(2,1)S(1)} %get-tuple-element.81), channel_id=1, source_target_pairs={{0,2},{2,4},{4,6},{6,8},{8,10},{10,12},{12,14},{1,3},{3,5},{5,7},{... | collective-permute-start | bytes 786440 | tf_op jit(solution)/shard_map/ppermute | solution.py:26
  89.4 16.2 %collective-permute-start.5 = (bf16[4,1,256,128]{3,2,1,0:T(8,128)(2,1)S(1)}, bf16[4,1,256,128]{3,2,1,0:T(8,128)(2,1)S(1)}, u32[]{:S(2)}, u32[]{:S(2)}) collective-permute-start(bf16[4,1,256,128]{3,2,1,0:T(8,128)(2,1)S(1)} %get-tuple-element.82), channel_id=1, source_target_pairs={{2,0},{4,2},{6,4},{8,6},{10,8},{12,10},{14,12},{3,1},{5,3},{7,5},{... | collective-permute-start | bytes 786440 | tf_op jit(solution)/shard_map/ppermute | solution.py:28
  109.8 1.0 copy-start
  109.8 0.9 copy-start.5
where the time goes:
time: 113 us; the launch traced here: 112 us
  blocking collectives  49.4 us (44%)
  waiting for transfers between devices  27.8 us (25%)
  starting transfers between devices  18.6 us (16%)
  matrix products  7.36 us (7%)
  local copies, waits for them, and re-layouts  4.33 us (4%)
  other arithmetic  3.9 us (3%)
    psum x2, blocking collectives, norm_stats(): totals, square_sums = lax.psum((sums, squares), ('tile', 'tm'))  49.4 us
    ppermute x2, waiting for transfers between devices, extended_2(): lax.ppermute(tail, axis, [(i, (i + 1) % count) for i in range(ends)])  20.3 us
    ppermute x2, starting transfers between devices, extended_2(): lax.ppermute(head, axis, [((i + 1) % count, i) for i in range(ends)])  11.9 us
    ppermute x2, waiting for transfers between devices, passed_along(): return lax.ppermute(x, axis, pairs)  7.49 us
    dot_general x18, matrix products, conv_block(): jnp.dot(stacked, kernel, preferred_element_type=jnp.float32)  7.36 us
    ppermute x2, starting transfers between devices, extended_2(): lax.ppermute(tail, axis, [(i, (i + 1) % count) for i in range(ends)])  3.84 us
    ppermute x2, starting transfers between devices, passed_along(): return lax.ppermute(x, axis, pairs)  2.85 us
    slice x5, local copies, waits for them, and re-layouts, conv_block(): window[:, :, col_tap:col_tap + col_count]  2.46 us
  transfers between devices with their start and end apart: 6, of which 4 were waited for; matrix products, arithmetic and copies ran while one was open for 0% of the time, Pallas kernels for 0%

commit v1 on v0

v1 whole, which is shorter than its diff:
```python
import functools

import jax
import jax.numpy as jnp
from jax import lax
from jax.experimental import pallas as pl
from jax.experimental.pallas import tpu as pltpu
from jax.sharding import PartitionSpec as P

G = 32
EPSILON = 1e-06
MESH = pl.DeviceIdType.MESH


def group_sums(x, width):
    lanes = x.shape[-1]
    lane = lax.broadcasted_iota(jnp.int32, x.shape, 1)
    step = 1
    while step < width:
        odd = (lane // step) % 2 == 1
        x = x + jnp.where(odd, pltpu.roll(x, step, 1), pltpu.roll(x, lanes - step, 1))
        step *= 2
    return x


def kernel(
    tiles,
    video,
    conv_first,
    conv_second,
    gain_first,
    shift_first,
    gain_second,
    shift_second,
    bias_second,
    out,
    raw,
    hid,
    taps,
    weight_first,
    weight_second,
    first_out,
    result,
    stat_mine,
    stat_got,
    local_sem,
    send_sem,
    recv_sem,
):
    count = tiles * 2
    tile, tm = lax.axis_index("tile"), lax.axis_index("tm")
    me = tile * 2 + tm
    cols, chans = raw.shape[2], raw.shape[3]
    cells = float(count * 4 * cols * (chans // G))
    has_up, has_down = tile > 0, tile < tiles - 1

    load_video = pltpu.make_async_copy(video, raw.at[pl.ds(2, 2), pl.ds(0, 2)], local_sem.at[0])
    load_first = pltpu.make_async_copy(conv_first, weight_first, local_sem.at[1])
    load_second = pltpu.make_async_copy(conv_second, weight_second, local_sem.at[2])
    load_video.start()
    load_first.start()
    load_second.start()

    def peer(k):
        other = lax.rem(me + k, count)
        return {"tile": other // 2, "tm": other % 2}

    barrier = pltpu.get_barrier_semaphore()

    @pl.loop(1, count)
    def _(k):
        pl.semaphore_signal(barrier, inc=1, device_id=peer(k), device_id_type=MESH)

    @pl.when(jnp.logical_not(has_up))
    def _():
        raw[:, 2] = jnp.zeros((4, cols, chans), jnp.bfloat16)
        hid[:, 2] = jnp.zeros((4, cols, chans), jnp.bfloat16)

    @pl.when(jnp.logical_not(has_down))
    def _():
        raw[:, 3] = jnp.zeros((4, cols, chans), jnp.bfloat16)
        hid[:, 3] = jnp.zeros((4, cols, chans), jnp.bfloat16)

    load_video.wait()

    def put_stats(phase, sums, squares):
        row = lax.broadcasted_iota(jnp.int32, (8, chans), 0)
        stat_mine[phase] = jnp.where(row == 0, sums, jnp.where(row == 1, squares, 0.0))

    def send_stats(phase):
        @pl.loop(1, count)
        def _(k):
            pltpu.make_async_remote_copy(
                src_ref=stat_mine.at[phase],
                dst_ref=stat_got.at[phase, k - 1],
                send_sem=send_sem.at[phase, 5],
                recv_sem=recv_sem.at[phase, 5],
                device_id=peer(k),
                device_id_type=MESH,
            ).start()

    def get_stats(phase, gain):
        got = stat_got.at[phase]
        pltpu.make_async_copy(got, got, recv_sem.at[phase, 5]).wait()
        total = group_sums(stat_mine[phase] + jnp.sum(stat_got[phase], axis=0), chans // G)
        mean = total[0:1] / cells
        spread = total[1:2] / cells - mean * mean
        return mean, lax.rsqrt(spread + EPSILON) * gain

    def copy_of(buf, phase, which):
        own = pl.ds(2, 2)
        src, dst, device = {
            "up": (buf.at[own, 0], buf.at[own, 3], {"tile": tile - 1, "tm": tm}),
            "down": (buf.at[own, 1], buf.at[own, 2], {"tile": tile + 1, "tm": tm}),
            "mate": (
                buf.at[own, pl.ds(0, 2)],
                buf.at[pl.ds(0, 2), pl.ds(0, 2)],
                {"tile": tile, "tm": 1 - tm},
            ),
            "mate_top": (buf.at[own, 2], buf.at[pl.ds(0, 2), 2], {"tile": tile, "tm": 1 - tm}),
            "mate_bottom": (buf.at[own, 3], buf.at[pl.ds(0, 2), 3], {"tile": tile, "tm": 1 - tm}),
        }[which]
        at = ("up", "down", "mate", "mate_top", "mate_bottom").index(which)
        return pltpu.make_async_remote_copy(
            src_ref=src,
            dst_ref=dst,
            send_sem=send_sem.at[phase, at],
            recv_sem=recv_sem.at[phase, at],
            device_id=device,
            device_id_type=MESH,
        )

    def send_edges(buf, phase):
        @pl.when(has_up)
        def _():
            copy_of(buf, phase, "up").start()

        @pl.when(has_down)
        def _():
            copy_of(buf, phase, "down").start()

        @pl.when(tm == 0)
        def _():
            copy_of(buf, phase, "mate").start()

    def wait_mate(buf, phase):
        @pl.when(tm == 1)
        def _():
            copy_of(buf, phase, "mate").wait_recv()

    def wait_edges(buf, phase):
        @pl.when(has_up)
        def _():
            copy_of(buf, phase, "down").wait_recv()

        @pl.when(tm == 0)
        def _():
            copy_of(buf, phase, "mate_top").start()

        @pl.when(has_down)
        def _():
            copy_of(buf, phase, "up").wait_recv()

        @pl.when(tm == 0)
        def _():
            copy_of(buf, phase, "mate_bottom").start()

    def wait_mate_edges(buf, phase):
        @pl.when(tm == 1)
        def _():
            copy_of(buf, phase, "mate_top").wait_recv()
            copy_of(buf, phase, "mate_bottom").wait_recv()

    def wait_sends(buf, phase):
        got = stat_got.at[phase]
        pltpu.make_async_copy(got, got, send_sem.at[phase, 5]).wait()

        @pl.when(has_up)
        def _():
            copy_of(buf, phase, "up").wait_send()

        @pl.when(has_down)
        def _():
            copy_of(buf, phase, "down").wait_send()

        @pl.when(tm == 0)
        def _():
            copy_of(buf, phase, "mate").wait_send()
            copy_of(buf, phase, "mate_top").wait_send()
            copy_of(buf, phase, "mate_bottom").wait_send()

    def normalized(values, mean, scale, shift):
        normed = (values - mean) * scale + shift
        return normed * (0.5 + 0.5 * jnp.tanh(0.5 * normed))

    row = lax.broadcasted_iota(jnp.int32, (cols, chans), 0)

    def put_taps(frame, slot, h):
        before = jnp.where(row == 0, 0.0, pltpu.roll(h, 1, 0))
        after = jnp.where(row == cols - 1, 0.0, pltpu.roll(h, cols - 1, 0))
        rows, base = pl.ds(frame * cols, cols), slot * 3 * chans
        taps[rows, base : base + chans] = before.astype(jnp.bfloat16)
        taps[rows, base + chans : base + 2 * chans] = h.astype(jnp.bfloat16)
        taps[rows, base + 2 * chans : base + 3 * chans] = after.astype(jnp.bfloat16)

    wide = 3 * chans
    none = jnp.zeros((wide, chans), jnp.bfloat16)

    def conv_part(weight, part):
        total = None
        for a in range(3):
            w = weight.at[a]
            if part == 0:
                kernel_a = jnp.concatenate([w[wide : 3 * wide], w[0 : 2 * wide]], axis=1)
            else:
                kernel_a = jnp.concatenate(
                    [
                        jnp.concatenate([w[0:wide], none], axis=0),
                        jnp.concatenate([none, w[2 * wide : 3 * wide]], axis=0),
                    ],
                    axis=1,
                )
            x = taps[a * cols : (a + 2) * cols, part * 2 * wide : (part + 1) * 2 * wide]
            y = jnp.dot(x, kernel_a, preferred_element_type=jnp.float32)
            total = y if total is None else total + y
        return total

    own = [(f, s) for f in (2, 3) for s in (0, 1)]
    past = [(f, s) for f in (0, 1) for s in (0, 1)]

    def source_frame(f):
        return jnp.where(tm == 0, 2, f) if f < 2 else f

    sums = jnp.zeros((1, chans), jnp.float32)
    squares = jnp.zeros((1, chans), jnp.float32)
    for f, s in own:
        values = raw[f, s].astype(jnp.float32)
        sums = sums + jnp.sum(values, axis=0, keepdims=True)
        squares = squares + jnp.sum(values * values, axis=0, keepdims=True)
    put_stats(0, sums, squares)
    pl.semaphore_wait(barrier, count - 1)
    send_stats(0)
    send_edges(raw, 0)

    mean, scale = get_stats(0, gain_first[...])
    shift = shift_first[...]

    def first_hidden(f, s):
        h = normalized(raw[source_frame(f), s].astype(jnp.float32), mean, scale, shift)
        if s == 2:
            h = jnp.where(has_up, h, 0.0)
        if s == 3:
            h = jnp.where(has_down, h, 0.0)
        put_taps(f, s, h)

    for f, s in own:
        first_hidden(f, s)
    wait_mate(raw, 0)
    for f, s in past:
        first_hidden(f, s)
    load_first.wait()
    first_out[...] = conv_part(weight_first, 0)
    wait_edges(raw, 0)
    for f in (2, 3):
        for s in (2, 3):
            first_hidden(f, s)
    wait_mate_edges(raw, 0)
    for f in (0, 1):
        for s in (2, 3):
            first_hidden(f, s)
    first = first_out[...] + conv_part(weight_first, 1)
    first_out[...] = first

    sums = jnp.sum(first, axis=0, keepdims=True)
    squares = jnp.sum(first * first, axis=0, keepdims=True)
    put_stats(1, sums[:, :chans] + sums[:, chans:], squares[:, :chans] + squares[:, chans:])
    send_stats(1)
    mean, scale = get_stats(1, gain_second[...])
    shift = shift_second[...]
    for f, s in own:
        h = normalized(
            first_out[(f - 2) * cols : (f - 1) * cols, s * chans : (s + 1) * chans],
            mean,
            scale,
            shift,
        )
        hid[f, s] = h.astype(jnp.bfloat16)
    send_edges(hid, 1)

    def second_hidden(f, s):
        put_taps(f, s, hid[source_frame(f), s].astype(jnp.float32))

    for f, s in own:
        second_hidden(f, s)
    wait_mate(hid, 1)
    for f, s in past:
        second_hidden(f, s)
    load_second.wait()
    first_out[...] = conv_part(weight_second, 0)
    wait_edges(hid, 1)
    for f in (2, 3):
        for s in (2, 3):
            second_hidden(f, s)
    wait_mate_edges(hid, 1)
    for f in (0, 1):
        for s in (2, 3):
            second_hidden(f, s)
    branch = first_out[...] + conv_part(weight_second, 1)
    bias = bias_second[...]
    for f, s in own:
        value = branch[(f - 2) * cols : (f - 1) * cols, s * chans : (s + 1) * chans]
        result[f - 2, s] = (raw[f, s].astype(jnp.float32) + value + bias).astype(jnp.bfloat16)
    store = pltpu.make_async_copy(result, out, local_sem.at[3])
    store.start()
    wait_sends(raw, 0)
    wait_sends(hid, 1)
    store.wait()


def solution(mesh):
    tiles = mesh.shape["tile"]
    count = tiles * mesh.shape["tm"]

    def step(video, conv_first, conv_second, *vectors):
        frames, rows, cols, chans = video.shape
        any_spec = pl.BlockSpec(memory_space=pl.ANY)
        vmem_spec = pl.BlockSpec(memory_space=pltpu.VMEM)
        bf16, f32 = jnp.bfloat16, jnp.float32
        return pl.pallas_call(
            functools.partial(kernel, tiles),
            out_shape=jax.ShapeDtypeStruct(video.shape, bf16),
            in_specs=[any_spec] * 3 + [vmem_spec] * 5,
            out_specs=any_spec,
            scratch_shapes=[
                pltpu.VMEM((frames + 2, rows + 2, cols, chans), bf16),
                pltpu.VMEM((frames + 2, rows + 2, cols, chans), bf16),
                pltpu.VMEM(((frames + 2) * cols, (rows + 2) * 3 * chans), bf16),
                pltpu.VMEM((3, 9 * chans, chans), bf16),
                pltpu.VMEM((3, 9 * chans, chans), bf16),
                pltpu.VMEM((frames * cols, rows * chans), f32),
                pltpu.VMEM(video.shape, bf16),
                pltpu.VMEM((2, 8, chans), f32),
                pltpu.VMEM((2, count - 1, 8, chans), f32),
                pltpu.SemaphoreType.DMA((4,)),
                pltpu.SemaphoreType.DMA((2, 6)),
                pltpu.SemaphoreType.DMA((2, 6)),
            ],
            compiler_params=pltpu.CompilerParams(
                collective_id=0, has_side_effects=True, vmem_limit_bytes=62 * 1024 * 1024
            ),
        )(
            video,
            conv_first.reshape(3, 9 * chans, chans),
            conv_second.reshape(3, 9 * chans, chans),
            *[v.reshape(1, chans) for v in vectors],
        )

    block = P(("grp", "tm"), "tile", None, None)
    return jax.shard_map(
        step, mesh=mesh, in_specs=(block,) + (P(),) * 7, out_specs=block, check_vma=False
    )
```

time: 113 us -> 32.1 us (0.28)
  blocking collectives: 49.4 us -> 0 us
  Pallas kernels: 0 us -> 30.2 us
  waiting for transfers between devices: 27.8 us -> 0 us
  starting transfers between devices: 18.6 us -> 0 us
  matrix products: 7.36 us -> 0 us
  other arithmetic: 3.9 us -> 0 us
  local copies, waits for them, and re-layouts: 4.33 us -> 1.67 us
    psum x2 -> x0, blocking collectives: 49.4 us -> none  [norm_stats(): totals, square_sums = lax.psum((sums, squares), ('tile', 'tm'))]
    pallas_call x0 -> x1, Pallas kernels: none -> 30.2 us  [step(): pl.pallas_call(functools.partial(kernel, tiles), out_shape=jax.ShapeDtype...]
    ppermute x6 -> x0, waiting for transfers between devices: 27.8 us -> none  [the longest x2 20.3 us: extended_2(): lax.ppermute(tail, axis, [(i, (i + 1) % count) for i in range(ends)])]
    ppermute x6 -> x0, starting transfers between devices: 18.6 us -> none  [the longest x2 11.9 us: extended_2(): lax.ppermute(head, axis, [((i + 1) % count, i) for i in range(ends)])]
    dot_general x18 -> x0, matrix products: 7.36 us -> none  [conv_block(): jnp.dot(stacked, kernel, preferred_element_type=jnp.float32)]
    slice x9 -> x0, local copies, waits for them, and re-layouts: 2.62 us -> none  [the longest x5 2.46 us: conv_block(): window[:, :, col_tap:col_tap + col_count]]
    reduce_sum x5 -> x0, other arithmetic: 1.56 us -> none  [the longest x3 1.33 us: norm_stats(): sums = jnp.sum(flat, axis=0).reshape(G, channels // G).sum(axis=1)]
    convert_element_type x2 -> x0, other arithmetic: 1.36 us -> none  [normalize(): return jax.nn.silu(normed).astype(jnp.bfloat16)]
  transfers between devices with their start and end apart: 6 -> 0, of which waited for: 4 -> 0; matrix products, arithmetic and copies ran while one was open for 0% -> 0% of each run, Pallas kernels for 0% -> 0%
where the time goes in v1:
time: 32.1 us; the launch traced here: 31.9 us
  Pallas kernels  30.2 us (94%)
  local copies, waits for them, and re-layouts  1.67 us (5%)
    pallas_call x1, Pallas kernels, step(): pl.pallas_call(functools.partial(kernel, tiles), out_shape=jax.ShapeDtype...  30.2 us
    unnamed x1, local copies, waits for them, and re-layouts  1.67 us

profile of v1, /device:TPU:3, one launch (start us, length us, event | category | flops | bytes accessed | tf_op | source)
XLA Modules:
  0.0 31.9 jit_solution(15481789391993223275)
XLA Ops:
  0.0 30.2 %shard_map.82 = bf16[2,2,256,128]{3,2,1,0:T(8,128)(2,1)} custom-call(bf16[2,2,256,128]{3,2,1,0:T(8,128)(2,1)} %video.1, bf16[3,1152,128]{2,1,0:T(8,128)(2,1)} %bitcast.7, bf16[3,1152,128]{2,1,0:T(8,128)(2,1)} %bitcast.8, f32[1,128]{1,0:T(1,128)} %bitcast.9, f32[1,128]{1,0:T(1,128)} %bitcast.10, f32[1,128]{1,0:T(1,128)} %bitcast.11, f32[1,128]{1,0:T(1,128)} %bitcast.12, ...), custom_call_target="tpu_custom_call" | custom-call | tf_op jit(solution)/shard_map/pallas_call | solution.py:329
  30.2 1.7 %copy.10 = bf16[2,2,256,128]{3,2,1,0:T(8,128)(2,1)} copy(bf16[2,2,256,128]{3,2,1,0:T(8,128)(2,1)} %shard_map.82) | data formatting | bytes 524288

commit v2 on v1

--- a/solution.py
+++ b/solution.py
@@ -49,7 +49,6 @@
 ):
     count = tiles * 2
     tile, tm = lax.axis_index("tile"), lax.axis_index("tm")
-    me = tile * 2 + tm
     cols, chans = raw.shape[2], raw.shape[3]
     cells = float(count * 4 * cols * (chans // G))
     has_up, has_down = tile > 0, tile < tiles - 1
@@ -61,15 +60,31 @@
     load_first.start()
     load_second.start()
 
-    def peer(k):
-        other = lax.rem(me + k, count)
-        return {"tile": other // 2, "tm": other % 2}
+    def peer(step, other_core):
+        other = tile + step
+        return {
+            "tile": jnp.where(other >= tiles, other - tiles, other),
+            "tm": 1 - tm if other_core else tm,
+        }
+
+    def each_peer(visit):
+        visit(0, {"tile": tile, "tm": 1 - tm})
+        for core in range(2):
+            if tiles <= 8:
+                for step in range(1, tiles):
+                    visit(2 * step - 1 + core, peer(step, core))
+            else:
+
+                @pl.loop(1, tiles)
+                def _(step):
+                    visit(2 * step - 1 + core, peer(step, core))
 
     barrier = pltpu.get_barrier_semaphore()
 
-    @pl.loop(1, count)
-    def _(k):
-        pl.semaphore_signal(barrier, inc=1, device_id=peer(k), device_id_type=MESH)
+    def greet(slot, device):
+        pl.semaphore_signal(barrier, inc=1, device_id=device, device_id_type=MESH)
+
+    each_peer(greet)
 
     @pl.when(jnp.logical_not(has_up))
     def _():
@@ -88,39 +103,39 @@
         stat_mine[phase] = jnp.where(row == 0, sums, jnp.where(row == 1, squares, 0.0))
 
     def send_stats(phase):
-        @pl.loop(1, count)
-        def _(k):
+        def send(slot, device):
             pltpu.make_async_remote_copy(
                 src_ref=stat_mine.at[phase],
-                dst_ref=stat_got.at[phase, k - 1],
-                send_sem=send_sem.at[phase, 5],
-                recv_sem=recv_sem.at[phase, 5],
-                device_id=peer(k),
+                dst_ref=stat_got.at[phase, slot],
+                send_sem=send_sem.at[phase, 10],
+                recv_sem=recv_sem.at[phase, 10],
+                device_id=device,
                 device_id_type=MESH,
             ).start()
 
+        each_peer(send)
+
     def get_stats(phase, gain):
         got = stat_got.at[phase]
-        pltpu.make_async_copy(got, got, recv_sem.at[phase, 5]).wait()
+        pltpu.make_async_copy(got, got, recv_sem.at[phase, 10]).wait()
         total = group_sums(stat_mine[phase] + jnp.sum(stat_got[phase], axis=0), chans // G)
         mean = total[0:1] / cells
         spread = total[1:2] / cells - mean * mean
         return mean, lax.rsqrt(spread + EPSILON) * gain
 
-    def copy_of(buf, phase, which):
-        own = pl.ds(2, 2)
+    def copy_of(buf, phase, which, f):
         src, dst, device = {
-            "up": (buf.at[own, 0], buf.at[own, 3], {"tile": tile - 1, "tm": tm}),
-            "down": (buf.at[own, 1], buf.at[own, 2], {"tile": tile + 1, "tm": tm}),
+            "up": (buf.at[2 + f, 0], buf.at[2 + f, 3], {"tile": tile - 1, "tm": tm}),
+            "down": (buf.at[2 + f, 1], buf.at[2 + f, 2], {"tile": tile + 1, "tm": tm}),
             "mate": (
-                buf.at[own, pl.ds(0, 2)],
-                buf.at[pl.ds(0, 2), pl.ds(0, 2)],
+                buf.at[2 + f, pl.ds(0, 2)],
+                buf.at[f, pl.ds(0, 2)],
                 {"tile": tile, "tm": 1 - tm},
             ),
-            "mate_top": (buf.at[own, 2], buf.at[pl.ds(0, 2), 2], {"tile": tile, "tm": 1 - tm}),
-            "mate_bottom": (buf.at[own, 3], buf.at[pl.ds(0, 2), 3], {"tile": tile, "tm": 1 - tm}),
+            "mate_top": (buf.at[2 + f, 2], buf.at[f, 2], {"tile": tile, "tm": 1 - tm}),
+            "mate_bottom": (buf.at[2 + f, 3], buf.at[f, 3], {"tile": tile, "tm": 1 - tm}),
         }[which]
-        at = ("up", "down", "mate", "mate_top", "mate_bottom").index(which)
+        at = ("up", "down", "mate", "mate_top", "mate_bottom").index(which) * 2 + f
         return pltpu.make_async_remote_copy(
             src_ref=src,
             dst_ref=dst,
@@ -130,64 +145,66 @@
             device_id_type=MESH,
         )
 
-    def send_edges(buf, phase):
+    def send_edges(buf, phase, f):
         @pl.when(has_up)
         def _():
-            copy_of(buf, phase, "up").start()
+            copy_of(buf, phase, "up", f).start()
 
         @pl.when(has_down)
         def _():
-            copy_of(buf, phase, "down").start()
+            copy_of(buf, phase, "down", f).start()
 
         @pl.when(tm == 0)
         def _():
-            copy_of(buf, phase, "mate").start()
+            copy_of(buf, phase, "mate", f).start()
 
     def wait_mate(buf, phase):
         @pl.when(tm == 1)
         def _():
-            copy_of(buf, phase, "mate").wait_recv()
-
-    def wait_edges(buf, phase):
+            for f in range(2):
+                copy_of(buf, phase, "mate", f).wait_recv()
+
+    def wait_edges(buf, phase, f):
         @pl.when(has_up)
         def _():
-            copy_of(buf, phase, "down").wait_recv()
+            copy_of(buf, phase, "down", f).wait_recv()
 
         @pl.when(tm == 0)
         def _():
-            copy_of(buf, phase, "mate_top").start()
+            copy_of(buf, phase, "mate_top", f).start()
 
         @pl.when(has_down)
         def _():
-            copy_of(buf, phase, "up").wait_recv()
+            copy_of(buf, phase, "up", f).wait_recv()
 
         @pl.when(tm == 0)
         def _():
-            copy_of(buf, phase, "mate_bottom").start()
-
-    def wait_mate_edges(buf, phase):
+            copy_of(buf, phase, "mate_bottom", f).start()
+
+    def wait_mate_edges(buf, phase, f):
         @pl.when(tm == 1)
         def _():
-            copy_of(buf, phase, "mate_top").wait_recv()
-            copy_of(buf, phase, "mate_bottom").wait_recv()
+            copy_of(buf, phase, "mate_top", f).wait_recv()
+            copy_of(buf, phase, "mate_bottom", f).wait_recv()
 
     def wait_sends(buf, phase):
         got = stat_got.at[phase]
-        pltpu.make_async_copy(got, got, send_sem.at[phase, 5]).wait()
-
-        @pl.when(has_up)
-        def _():
-            copy_of(buf, phase, "up").wait_send()
-
-        @pl.when(has_down)
-        def _():
-            copy_of(buf, phase, "down").wait_send()
-
-        @pl.when(tm == 0)
-        def _():
-            copy_of(buf, phase, "mate").wait_send()
-            copy_of(buf, phase, "mate_top").wait_send()
-            copy_of(buf, phase, "mate_bottom").wait_send()
+        pltpu.make_async_copy(got, got, send_sem.at[phase, 10]).wait()
+        for f in range(2):
+
+            @pl.when(has_up)
+            def _():
+                copy_of(buf, phase, "up", f).wait_send()
+
+            @pl.when(has_down)
+            def _():
+                copy_of(buf, phase, "down", f).wait_send()
+
+            @pl.when(tm == 0)
+            def _():
+                copy_of(buf, phase, "mate", f).wait_send()
+                copy_of(buf, phase, "mate_top", f).wait_send()
+                copy_of(buf, phase, "mate_bottom", f).wait_send()
 
     def normalized(values, mean, scale, shift):
         normed = (values - mean) * scale + shift
@@ -240,7 +257,8 @@
     put_stats(0, sums, squares)
     pl.semaphore_wait(barrier, count - 1)
     send_stats(0)
-    send_edges(raw, 0)
+    for f in range(2):
+        send_edges(raw, 0, f)
 
     mean, scale = get_stats(0, gain_first[...])
     shift = shift_first[...]
@@ -260,12 +278,13 @@
         first_hidden(f, s)
     load_first.wait()
     first_out[...] = conv_part(weight_first, 0)
-    wait_edges(raw, 0)
-    for f in (2, 3):
+    for f in range(2):
+        wait_edges(raw, 0, f)
+    for f in range(2):
         for s in (2, 3):
-            first_hidden(f, s)
-    wait_mate_edges(raw, 0)
-    for f in (0, 1):
+            first_hidden(f + 2, s)
+    for f in range(2):
+        wait_mate_edges(raw, 0, f)
         for s in (2, 3):
             first_hidden(f, s)
     first = first_out[...] + conv_part(weight_first, 1)
@@ -285,7 +304,8 @@
             shift,
         )
         hid[f, s] = h.astype(jnp.bfloat16)
-    send_edges(hid, 1)
+        if s == 1:
+            send_edges(hid, 1, f - 2)
 
     def second_hidden(f, s):
         put_taps(f, s, hid[source_frame(f), s].astype(jnp.float32))
@@ -297,12 +317,13 @@
         second_hidden(f, s)
     load_second.wait()
     first_out[...] = conv_part(weight_second, 0)
-    wait_edges(hid, 1)
-    for f in (2, 3):
+    for f in range(2):
+        wait_edges(hid, 1, f)
+    for f in range(2):
         for s in (2, 3):
-            second_hidden(f, s)
-    wait_mate_edges(hid, 1)
-    for f in (0, 1):
+            second_hidden(f + 2, s)
+    for f in range(2):
+        wait_mate_edges(hid, 1, f)
         for s in (2, 3):
             second_hidden(f, s)
     branch = first_out[...] + conv_part(weight_second, 1)
@@ -342,8 +363,8 @@
                 pltpu.VMEM((2, 8, chans), f32),
                 pltpu.VMEM((2, count - 1, 8, chans), f32),
                 pltpu.SemaphoreType.DMA((4,)),
-                pltpu.SemaphoreType.DMA((2, 6)),
-                pltpu.SemaphoreType.DMA((2, 6)),
+                pltpu.SemaphoreType.DMA((2, 11)),
+                pltpu.SemaphoreType.DMA((2, 11)),
             ],
             compiler_params=pltpu.CompilerParams(
                 collective_id=0, has_side_effects=True, vmem_limit_bytes=62 * 1024 * 1024

time: 32.1 us -> 31.6 us (0.984)
  Pallas kernels: 30.2 us -> 29.7 us
    pallas_call x1, Pallas kernels: 30.2 us -> 29.7 us  [step(): pl.pallas_call(functools.partial(kernel, tiles), out_shape=jax.ShapeDtype...]
where the time goes in v2:
time: 31.6 us; the launch traced here: 31.4 us
  Pallas kernels  29.7 us (94%)
  local copies, waits for them, and re-layouts  1.67 us (5%)
    pallas_call x1, Pallas kernels, step(): pl.pallas_call(functools.partial(kernel, tiles), out_shape=jax.ShapeDtype...  29.7 us
    unnamed x1, local copies, waits for them, and re-layouts  1.67 us

profile of v2, /device:TPU:3, one launch (start us, length us, event | category | flops | bytes accessed | tf_op | source)
XLA Modules:
  0.0 31.4 jit_solution(18291323579266270997)
XLA Ops:
  0.0 29.7 %shard_map.82 = bf16[2,2,256,128]{3,2,1,0:T(8,128)(2,1)} custom-call(bf16[2,2,256,128]{3,2,1,0:T(8,128)(2,1)} %video.1, bf16[3,1152,128]{2,1,0:T(8,128)(2,1)} %bitcast.7, bf16[3,1152,128]{2,1,0:T(8,128)(2,1)} %bitcast.8, f32[1,128]{1,0:T(1,128)} %bitcast.9, f32[1,128]{1,0:T(1,128)} %bitcast.10, f32[1,128]{1,0:T(1,128)} %bitcast.11, f32[1,128]{1,0:T(1,128)} %bitcast.12, ...), custom_call_target="tpu_custom_call" | custom-call | tf_op jit(solution)/shard_map/pallas_call | solution.py:350
  29.7 1.7 %copy.10 = bf16[2,2,256,128]{3,2,1,0:T(8,128)(2,1)} copy(bf16[2,2,256,128]{3,2,1,0:T(8,128)(2,1)} %shard_map.82) | data formatting | bytes 524288

commit v3 on v2

--- a/solution.py
+++ b/solution.py
@@ -223,9 +223,9 @@
     wide = 3 * chans
     none = jnp.zeros((wide, chans), jnp.bfloat16)
 
-    def conv_part(weight, part):
+    def conv_part(weight, part, times):
         total = None
-        for a in range(3):
+        for a in times:
             w = weight.at[a]
             if part == 0:
                 kernel_a = jnp.concatenate([w[wide : 3 * wide], w[0 : 2 * wide]], axis=1)
@@ -273,21 +273,23 @@
 
     for f, s in own:
         first_hidden(f, s)
+    load_first.wait()
+    first_out[...] = conv_part(weight_first, 0, (2,))
     wait_mate(raw, 0)
     for f, s in past:
         first_hidden(f, s)
-    load_first.wait()
-    first_out[...] = conv_part(weight_first, 0)
+    first_out[...] = first_out[...] + conv_part(weight_first, 0, (0, 1))
     for f in range(2):
         wait_edges(raw, 0, f)
     for f in range(2):
         for s in (2, 3):
             first_hidden(f + 2, s)
+    first_out[...] = first_out[...] + conv_part(weight_first, 1, (2,))
     for f in range(2):
         wait_mate_edges(raw, 0, f)
         for s in (2, 3):
             first_hidden(f, s)
-    first = first_out[...] + conv_part(weight_first, 1)
+    first = first_out[...] + conv_part(weight_first, 1, (0, 1))
     first_out[...] = first
 
     sums = jnp.sum(first, axis=0, keepdims=True)
@@ -312,21 +314,23 @@
 
     for f, s in own:
         second_hidden(f, s)
+    load_second.wait()
+    first_out[...] = conv_part(weight_second, 0, (2,))
     wait_mate(hid, 1)
     for f, s in past:
         second_hidden(f, s)
-    load_second.wait()
-    first_out[...] = conv_part(weight_second, 0)
+    first_out[...] = first_out[...] + conv_part(weight_second, 0, (0, 1))
     for f in range(2):
         wait_edges(hid, 1, f)
     for f in range(2):
         for s in (2, 3):
             second_hidden(f + 2, s)
+    first_out[...] = first_out[...] + conv_part(weight_second, 1, (2,))
     for f in range(2):
         wait_mate_edges(hid, 1, f)
         for s in (2, 3):
             second_hidden(f, s)
-    branch = first_out[...] + conv_part(weight_second, 1)
+    branch = first_out[...] + conv_part(weight_second, 1, (0, 1))
     bias = bias_second[...]
     for f, s in own:
         value = branch[(f - 2) * cols : (f - 1) * cols, s * chans : (s + 1) * chans]

time: 31.6 us -> 31.1 us (0.984)
  Pallas kernels: 29.7 us -> 29.3 us
    pallas_call x1, Pallas kernels: 29.7 us -> 29.3 us  [step(): pl.pallas_call(functools.partial(kernel, tiles), out_shape=jax.ShapeDtype...]
where the time goes in v3:
time: 31.1 us; the launch traced here: 31 us
  Pallas kernels  29.3 us (94%)
  local copies, waits for them, and re-layouts  1.67 us (5%)
    pallas_call x1, Pallas kernels, step(): pl.pallas_call(functools.partial(kernel, tiles), out_shape=jax.ShapeDtype...  29.3 us
    unnamed x1, local copies, waits for them, and re-layouts  1.67 us

profile of v3, /device:TPU:3, one launch (start us, length us, event | category | flops | bytes accessed | tf_op | source)
XLA Modules:
  0.0 31.0 jit_solution(12415893531948773405)
XLA Ops:
  0.0 29.3 %shard_map.82 = bf16[2,2,256,128]{3,2,1,0:T(8,128)(2,1)} custom-call(bf16[2,2,256,128]{3,2,1,0:T(8,128)(2,1)} %video.1, bf16[3,1152,128]{2,1,0:T(8,128)(2,1)} %bitcast.7, bf16[3,1152,128]{2,1,0:T(8,128)(2,1)} %bitcast.8, f32[1,128]{1,0:T(1,128)} %bitcast.9, f32[1,128]{1,0:T(1,128)} %bitcast.10, f32[1,128]{1,0:T(1,128)} %bitcast.11, f32[1,128]{1,0:T(1,128)} %bitcast.12, ...), custom_call_target="tpu_custom_call" | custom-call | tf_op jit(solution)/shard_map/pallas_call | solution.py:354
  29.3 1.7 %copy.10 = bf16[2,2,256,128]{3,2,1,0:T(8,128)(2,1)} copy(bf16[2,2,256,128]{3,2,1,0:T(8,128)(2,1)} %shard_map.82) | data formatting | bytes 524288

commit v4 on v3

--- a/solution.py
+++ b/solution.py
@@ -281,7 +281,6 @@
     first_out[...] = first_out[...] + conv_part(weight_first, 0, (0, 1))
     for f in range(2):
         wait_edges(raw, 0, f)
-    for f in range(2):
         for s in (2, 3):
             first_hidden(f + 2, s)
     first_out[...] = first_out[...] + conv_part(weight_first, 1, (2,))
@@ -322,7 +321,6 @@
     first_out[...] = first_out[...] + conv_part(weight_second, 0, (0, 1))
     for f in range(2):
         wait_edges(hid, 1, f)
-    for f in range(2):
         for s in (2, 3):
             second_hidden(f + 2, s)
     first_out[...] = first_out[...] + conv_part(weight_second, 1, (2,))

time: 31.1 us -> 31.1 us (level)
  no operation moved by 1% of the time
where the time goes in v4:
time: 31.1 us; the launch traced here: 30.9 us
  Pallas kernels  29.3 us (94%)
  local copies, waits for them, and re-layouts  1.67 us (5%)
    pallas_call x1, Pallas kernels, step(): pl.pallas_call(functools.partial(kernel, tiles), out_shape=jax.ShapeDtype...  29.3 us
    unnamed x1, local copies, waits for them, and re-layouts  1.67 us

profile of v4, /device:TPU:3, one launch (start us, length us, event | category | flops | bytes accessed | tf_op | source)
XLA Modules:
  0.0 30.9 jit_solution(14683681053584635691)
XLA Ops:
  0.0 29.3 %shard_map.82 = bf16[2,2,256,128]{3,2,1,0:T(8,128)(2,1)} custom-call(bf16[2,2,256,128]{3,2,1,0:T(8,128)(2,1)} %video.1, bf16[3,1152,128]{2,1,0:T(8,128)(2,1)} %bitcast.7, bf16[3,1152,128]{2,1,0:T(8,128)(2,1)} %bitcast.8, f32[1,128]{1,0:T(1,128)} %bitcast.9, f32[1,128]{1,0:T(1,128)} %bitcast.10, f32[1,128]{1,0:T(1,128)} %bitcast.11, f32[1,128]{1,0:T(1,128)} %bitcast.12, ...), custom_call_target="tpu_custom_call" | custom-call | tf_op jit(solution)/shard_map/pallas_call | solution.py:352
  29.3 1.7 %copy.10 = bf16[2,2,256,128]{3,2,1,0:T(8,128)(2,1)} copy(bf16[2,2,256,128]{3,2,1,0:T(8,128)(2,1)} %shard_map.82) | data formatting | bytes 524288

commit v5 on v3

--- a/solution.py
+++ b/solution.py
@@ -57,8 +57,6 @@
     load_first = pltpu.make_async_copy(conv_first, weight_first, local_sem.at[1])
     load_second = pltpu.make_async_copy(conv_second, weight_second, local_sem.at[2])
     load_video.start()
-    load_first.start()
-    load_second.start()
 
     def peer(step, other_core):
         other = tile + step
@@ -85,6 +83,8 @@
         pl.semaphore_signal(barrier, inc=1, device_id=device, device_id_type=MESH)
 
     each_peer(greet)
+    load_first.start()
+    load_second.start()
 
     @pl.when(jnp.logical_not(has_up))
     def _():
@@ -332,14 +332,18 @@
             second_hidden(f, s)
     branch = first_out[...] + conv_part(weight_second, 1, (0, 1))
     bias = bias_second[...]
+    stores = [
+        pltpu.make_async_copy(result.at[f], out.at[f], local_sem.at[3 + f]) for f in range(2)
+    ]
     for f, s in own:
         value = branch[(f - 2) * cols : (f - 1) * cols, s * chans : (s + 1) * chans]
         result[f - 2, s] = (raw[f, s].astype(jnp.float32) + value + bias).astype(jnp.bfloat16)
-    store = pltpu.make_async_copy(result, out, local_sem.at[3])
-    store.start()
+        if s == 1:
+            stores[f - 2].start()
     wait_sends(raw, 0)
     wait_sends(hid, 1)
-    store.wait()
+    for store in stores:
+        store.wait()
 
 
 def solution(mesh):
@@ -366,7 +370,7 @@
                 pltpu.VMEM(video.shape, bf16),
                 pltpu.VMEM((2, 8, chans), f32),
                 pltpu.VMEM((2, count - 1, 8, chans), f32),
-                pltpu.SemaphoreType.DMA((4,)),
+                pltpu.SemaphoreType.DMA((5,)),
                 pltpu.SemaphoreType.DMA((2, 11)),
                 pltpu.SemaphoreType.DMA((2, 11)),
             ],

time: 31.1 us -> 31.1 us (level)
  no operation moved by 1% of the time
where the time goes in v5:
time: 31.1 us; the launch traced here: 30.9 us
  Pallas kernels  29.3 us (94%)
  local copies, waits for them, and re-layouts  1.67 us (5%)
    pallas_call x1, Pallas kernels, step(): pl.pallas_call(functools.partial(kernel, tiles), out_shape=jax.ShapeDtype...  29.3 us
    unnamed x1, local copies, waits for them, and re-layouts  1.67 us

profile of v5, /device:TPU:3, one launch (start us, length us, event | category | flops | bytes accessed | tf_op | source)
XLA Modules:
  0.0 30.9 jit_solution(8870811324175664281)
XLA Ops:
  0.0 29.3 %shard_map.82 = bf16[2,2,256,128]{3,2,1,0:T(8,128)(2,1)} custom-call(bf16[2,2,256,128]{3,2,1,0:T(8,128)(2,1)} %video.1, bf16[3,1152,128]{2,1,0:T(8,128)(2,1)} %bitcast.7, bf16[3,1152,128]{2,1,0:T(8,128)(2,1)} %bitcast.8, f32[1,128]{1,0:T(1,128)} %bitcast.9, f32[1,128]{1,0:T(1,128)} %bitcast.10, f32[1,128]{1,0:T(1,128)} %bitcast.11, f32[1,128]{1,0:T(1,128)} %bitcast.12, ...), custom_call_target="tpu_custom_call" | custom-call | tf_op jit(solution)/shard_map/pallas_call | solution.py:358
  29.3 1.7 %copy.10 = bf16[2,2,256,128]{3,2,1,0:T(8,128)(2,1)} copy(bf16[2,2,256,128]{3,2,1,0:T(8,128)(2,1)} %shard_map.82) | data formatting | bytes 524288

commit v6 on v5

--- a/solution.py
+++ b/solution.py
@@ -121,7 +121,7 @@
         total = group_sums(stat_mine[phase] + jnp.sum(stat_got[phase], axis=0), chans // G)
         mean = total[0:1] / cells
         spread = total[1:2] / cells - mean * mean
-        return mean, lax.rsqrt(spread + EPSILON) * gain
+        return mean, lax.rsqrt(spread + EPSILON) * (0.5 * gain)
 
     def copy_of(buf, phase, which, f):
         src, dst, device = {
@@ -207,8 +207,8 @@
                 copy_of(buf, phase, "mate_bottom", f).wait_send()
 
     def normalized(values, mean, scale, shift):
-        normed = (values - mean) * scale + shift
-        return normed * (0.5 + 0.5 * jnp.tanh(0.5 * normed))
+        half = (values - mean) * scale + shift
+        return half + half * jnp.tanh(half)
 
     row = lax.broadcasted_iota(jnp.int32, (cols, chans), 0)
 
@@ -261,7 +261,7 @@
         send_edges(raw, 0, f)
 
     mean, scale = get_stats(0, gain_first[...])
-    shift = shift_first[...]
+    shift = 0.5 * shift_first[...]
 
     def first_hidden(f, s):
         h = normalized(raw[source_frame(f), s].astype(jnp.float32), mean, scale, shift)
@@ -297,7 +297,7 @@
     put_stats(1, sums[:, :chans] + sums[:, chans:], squares[:, :chans] + squares[:, chans:])
     send_stats(1)
     mean, scale = get_stats(1, gain_second[...])
-    shift = shift_second[...]
+    shift = 0.5 * shift_second[...]
     for f, s in own:
         h = normalized(
             first_out[(f - 2) * cols : (f - 1) * cols, s * chans : (s + 1) * chans],

time: 31.1 us -> 31.1 us (level)
  no operation moved by 1% of the time
where the time goes in v6:
time: 31.1 us; the launch traced here: 30.9 us
  Pallas kernels  29.2 us (94%)
  local copies, waits for them, and re-layouts  1.67 us (5%)
    pallas_call x1, Pallas kernels, step(): pl.pallas_call(functools.partial(kernel, tiles), out_shape=jax.ShapeDtype...  29.2 us
    unnamed x1, local copies, waits for them, and re-layouts  1.67 us

profile of v6, /device:TPU:3, one launch (start us, length us, event | category | flops | bytes accessed | tf_op | source)
XLA Modules:
  0.0 30.9 jit_solution(5730818747662761101)
XLA Ops:
  0.0 29.2 %shard_map.82 = bf16[2,2,256,128]{3,2,1,0:T(8,128)(2,1)} custom-call(bf16[2,2,256,128]{3,2,1,0:T(8,128)(2,1)} %video.1, bf16[3,1152,128]{2,1,0:T(8,128)(2,1)} %bitcast.7, bf16[3,1152,128]{2,1,0:T(8,128)(2,1)} %bitcast.8, f32[1,128]{1,0:T(1,128)} %bitcast.9, f32[1,128]{1,0:T(1,128)} %bitcast.10, f32[1,128]{1,0:T(1,128)} %bitcast.11, f32[1,128]{1,0:T(1,128)} %bitcast.12, ...), custom_call_target="tpu_custom_call" | custom-call | tf_op jit(solution)/shard_map/pallas_call | solution.py:358
  29.2 1.7 %copy.10 = bf16[2,2,256,128]{3,2,1,0:T(8,128)(2,1)} copy(bf16[2,2,256,128]{3,2,1,0:T(8,128)(2,1)} %shard_map.82) | data formatting | bytes 524288
